TPU v7x, 128 devices: a whole 4x4x4 slice. The times are simulated.
128 devices in a mesh: leaf: 128 (over x, z, y, core).
Axes of the slice: x: 4, y: 4, z: 4, core: 2. Of those that a mesh axis runs over, the one named last changes fastest.
Arguments:
- points: float32 [131072, 64], P('leaf'), may hold values from -6 to 6
- coefficients: float32 [131072, 256], P('leaf'), may hold values from -6 to 6
- leaf_skeleton: int32 [256, 256], P('leaf'), may hold values from 0 to 511, as said below
- node_skeleton: int32 [128, 256], P('leaf'), may hold values from 0 to 511, as said below
- pair_skeleton: int32 [64, 256], replicated, may hold values from 0 to 511, as said below
- quad_skeleton: int32 [32, 256], replicated, may hold values from 0 to 511, as said below
- top_skeleton: int32 [16, 256], replicated, may hold values from 0 to 511, as said below
- near_list: int32 [256, 3], P('leaf'), may hold values from -1 to 255, as said below
- far_list: int32 [128, 3], P('leaf'), may hold values from -1 to 127, as said below
- top_far_list: int32 [16, 3], replicated, may hold values from 0 to 15, as said below
Outputs:
- potential: float32 [131072, 256], P('leaf')
Inputs may be any that keep to these rules, and one draw needn't show every extreme that they name: `leaf_skeleton`: each row holds 256 distinct rows of its leaf. `node_skeleton`: each row holds 256 distinct candidate rows. `pair_skeleton`: each row holds 256 distinct candidate rows. `quad_skeleton`: each row holds 256 distinct candidate rows. `top_skeleton`: each row holds 256 distinct candidate rows. `near_list`: row l names leaf l first; each other slot names a distinct leaf j with 1 <= |j - l| <= 2, or is -1. `far_list`: each slot names a distinct node m with 2 <= |m - n| <= 4, or is -1. `top_far_list`: each row names 3 distinct top nodes other than its own.
All inputs are finite; a program needn't handle non-finite values.
Results may differ from a plain program's by a relative error of at most 0.0003.
Values sent between devices are 32-bit elements; how exact they have to be, the bound alone decides.
A program may use at most 128 MiB of HBM per device.

v0:
```python
import math

import jax
import jax.numpy as jnp
from jax import lax
from jax.experimental import pallas as pl
from jax.experimental.pallas import tpu as pltpu
from jax.sharding import PartitionSpec as P

FEAT = 64
RHS = 256
RANK = 256
LEAF = 512
NEAR = 3
FAR1 = 3
FAR4 = 3
GROUP = 8
TOPS = 16
DEVICES = 128
SHARE = RHS // GROUP
HALF = RANK // 2

MESH = pl.DeviceIdType.MESH
F32 = jnp.float32
BF16 = jnp.bfloat16
SCALE = math.sqrt(2.0 * math.log2(math.e) / FEAT)


def dot(left, right, dims):
    return lax.dot_general(left, right, (dims, ((), ())), preferred_element_type=F32)


def nn(left, right):
    return dot(left, right, ((1,), (0,)))


def nt(left, right):
    return dot(left, right, ((1,), (1,)))


def tn(left, right):
    return dot(left, right, ((0,), (0,)))


def split(values):
    high = values.astype(BF16)
    low = (values - high.astype(F32)).astype(BF16)
    return high, low


def product3(mul, left, right):
    return mul(left[0], right[0]) + (mul(left[0], right[1]) + mul(left[1], right[0]))


def thin_product(mul, left, right):
    rows = left.shape[0]
    high, low = split(left)
    both = mul(jnp.concatenate([high, low], axis=0), right[0])
    return both[:rows] + (both[rows:] + mul(high, right[1]))


def lanes_of(shape):
    return lax.broadcasted_iota(jnp.int32, shape, 1)


def swap_halves(tile):
    return pltpu.roll(tile, FEAT, 1)


def doubled(packed):
    lane = lanes_of(packed.shape)
    swapped = swap_halves(packed)
    return jnp.concatenate(
        [jnp.where(lane < FEAT, packed, swapped), jnp.where(lane < FEAT, swapped, packed)], axis=0
    )


def forms(twice):
    lane = lanes_of(twice.shape)
    first = lane < FEAT
    high = twice.astype(BF16).astype(F32)
    low = twice - high
    norm = -0.25 * jnp.sum(twice * twice, axis=1, keepdims=True)
    norm1 = norm.astype(BF16).astype(F32)
    norm2 = (norm - norm1).astype(BF16).astype(F32)
    norm3 = norm - norm1 - norm2

    def placed(base):
        return jnp.where(
            lane == base, norm1, jnp.where(lane == base + 1, norm2, jnp.where(lane == base + 2, norm3, 0.0))
        )

    ones_left = jnp.where((lane >= FEAT + 3) & (lane < FEAT + 6), 1.0, placed(FEAT))
    ones_right = jnp.where((lane >= FEAT) & (lane < FEAT + 3), 1.0, placed(FEAT + 3))
    left = jnp.concatenate(
        [jnp.where(first, high, low).astype(BF16), jnp.where(first, high, ones_left).astype(BF16)], axis=1
    )
    right = jnp.concatenate(
        [jnp.where(first, low, high).astype(BF16), jnp.where(first, high, ones_right).astype(BF16)], axis=1
    )
    return left, right


def picked_forms(picked):
    head, tail = picked[:, :128], picked[:, 128:]
    lane = lanes_of(head.shape)
    swapped = swap_halves(head)
    moved = pltpu.roll(tail, 3, 1)
    tail_right = jnp.where(
        lane < FEAT,
        tail,
        jnp.where(lane < FEAT + 3, 1.0, jnp.where(lane < FEAT + 6, moved, 0.0)),
    )
    right = jnp.concatenate([swapped.astype(BF16), tail_right.astype(BF16)], axis=1)
    return picked.astype(BF16), right, head + swapped


def one_hot(column):
    spread = lax.broadcasted_iota(jnp.int32, (RANK, 2 * RANK), 1)
    return jnp.where(spread == column, 1.0, 0.0).astype(BF16)


def softmax3(exponent):
    top = jnp.max(exponent, axis=1, keepdims=True)
    weights = jnp.exp2(3.0 * (exponent - top))
    return weights / jnp.sum(weights, axis=1, keepdims=True)


def kernel(
    near_list,
    far_list,
    top_far_list,
    points,
    coefficients,
    leaf_skeleton,
    node_skeleton,
    pair_skeleton,
    quad_skeleton,
    top_skeleton,
    out,
    near_send_points,
    near_points,
    near_values,
    node_points,
    node_values,
    node_lists,
    list_scalars,
    top_points,
    top_values,
    field_out,
    field_in,
    weights_t,
    index_rows,
    index_columns,
    leaf_left,
    near_right,
    values_high,
    values_low,
    basis_high,
    basis_low,
    node_left,
    node_right,
    upper_left,
    upper_right,
    pair_high,
    pair_low,
    chain_high,
    chain_low,
    near_send,
    near_recv,
    gpts_send,
    gpts_recv,
    glist_send,
    glist_recv,
    gval_send,
    gval_recv,
    edge_send,
    edge_recv,
    tpts_send,
    tpts_recv,
    tval_send,
    tval_recv,
    back_send,
    back_recv,
    local_sem,
):
    me = lax.axis_index("leaf")
    place = lax.rem(me, GROUP)
    group = me // GROUP
    right_device = lax.rem(me + 1, DEVICES)
    left_device = lax.rem(me + DEVICES - 1, DEVICES)
    next_group = lax.rem(group + 1, TOPS) * GROUP + place
    previous_group = lax.rem(group + TOPS - 1, TOPS) * GROUP + place

    def mate(step):
        return group * GROUP + lax.rem(place + step, GROUP)

    def peer(step):
        return lax.rem(group + step, TOPS) * GROUP + place

    barrier = pltpu.get_barrier_semaphore()
    partners = [right_device, left_device]
    partners += [mate(step) for step in range(1, GROUP)]
    partners += [peer(step) for step in range(1, TOPS)]
    for partner in partners:
        pl.semaphore_signal(barrier, inc=1, device_id=(partner,), device_id_type=MESH)

    def remote(source, target, send, recv, device):
        return pltpu.make_async_remote_copy(
            src_ref=source, dst_ref=target, send_sem=send, recv_sem=recv, device_id=(device,), device_id_type=MESH
        )

    started = []

    def start(*args):
        copy = remote(*args)
        copy.start()
        started.append(copy)

    near_send_points[...] = jnp.concatenate([points[0:LEAF, :], points[LEAF : 2 * LEAF, :]], axis=1) * SCALE
    pl.semaphore_wait(barrier, len(partners))

    def near_copies():
        copies = []
        for side, device in ((0, right_device), (1, left_device)):
            copies.append((near_send_points, near_points.at[side], near_send.at[side, 0], near_recv.at[side, 0], device))
            for part in range(4):
                rows = pl.ds(part * 256, 256)
                copies.append(
                    (
                        coefficients.at[rows, :],
                        near_values.at[side, rows, :],
                        near_send.at[side, part + 1],
                        near_recv.at[side, part + 1],
                        device,
                    )
                )
        return copies

    for copy in near_copies():
        start(*copy)

    index_rows[...] = jnp.zeros_like(index_rows)
    index_rows[0:2, :] = leaf_skeleton[...].astype(F32)
    index_rows[2:3, :] = node_skeleton[...].astype(F32)
    for i in range(4):
        index_rows[3 + i : 4 + i, :] = pair_skeleton[pl.ds(group * 4 + i, 1), :].astype(F32)
    for i in range(2):
        index_rows[7 + i : 8 + i, :] = quad_skeleton[pl.ds(group * 2 + i, 1), :].astype(F32)
    index_rows[9:10, :] = top_skeleton[pl.ds(group, 1), :].astype(F32)
    index_columns[...] = jnp.transpose(index_rows[...]).astype(jnp.int32)

    def chosen(number):
        return one_hot(index_columns[:, number : number + 1])

    leaf_picks = []
    for leaf in range(2):
        packed = near_send_points[...]
        lane = lanes_of(packed.shape)
        swapped = swap_halves(packed)
        twice = jnp.where(lane < FEAT, packed, swapped) if leaf == 0 else jnp.where(lane < FEAT, swapped, packed)
        left, right = forms(twice)
        leaf_left[leaf * LEAF : (leaf + 1) * LEAF, :] = left
        near_right[2 + leaf] = right
        pick_left, pick_right, _ = picked_forms(nn(chosen(leaf), left))
        upper_left[leaf * RANK : (leaf + 1) * RANK, :] = pick_left
        upper_right[leaf * RANK : (leaf + 1) * RANK, :] = pick_right
    _, node_pick_right, node_twice = picked_forms(nn(chosen(2), upper_left[0 : 2 * RANK, :]))
    lane = lanes_of((HALF, 128))
    node_points[4 + place] = jnp.where(lane < FEAT, node_twice[:HALF], node_twice[HALF:])
    lane_row = lanes_of((1, 128))
    node_lists[place] = jnp.where(
        lane_row == 0, far_list[0, 0], jnp.where(lane_row == 1, far_list[0, 1], far_list[0, 2])
    )
    for step in range(1, GROUP):
        start(
            node_points.at[4 + place], node_points.at[4 + place], gpts_send.at[step], gpts_recv.at[step], mate(step)
        )
    for step in range(1, GROUP):
        start(node_lists.at[place], node_lists.at[place], glist_send.at[step], glist_recv.at[step], mate(step))

    for leaf in range(2):
        rows = slice(leaf * LEAF, (leaf + 1) * LEAF)
        picks = slice(leaf * RANK, (leaf + 1) * RANK)
        basis = softmax3(nt(leaf_left[rows, :], upper_right[picks, :]))
        transfer = softmax3(nt(upper_left[picks, :], node_pick_right))
        high, low = split(product3(nn, split(basis), split(transfer)))
        basis_high[rows, :] = high
        basis_low[rows, :] = low
        high, low = split(coefficients[rows, :])
        values_high[2 + leaf] = high
        values_low[2 + leaf] = low
    weights = product3(
        tn,
        (values_high[2:4].reshape(2 * LEAF, RHS), values_low[2:4].reshape(2 * LEAF, RHS)),
        (basis_high[...], basis_low[...]),
    )
    weights_t[...] = weights.reshape(GROUP, SHARE, RANK)
    for step in range(1, GROUP):
        start(
            weights_t.at[lax.rem(place + step, GROUP)],
            node_values.at[4 + place],
            gval_send.at[step],
            gval_recv.at[step],
            mate(step),
        )
    node_values[4 + place] = weights_t[place]

    for step in range(1, GROUP):
        source = 4 + lax.rem(place + GROUP - step, GROUP)
        remote(
            node_points.at[source], node_points.at[source], gpts_send.at[step], gpts_recv.at[step], mate(step)
        ).wait_recv()
    start(node_points.at[pl.ds(8, 4)], node_points.at[pl.ds(0, 4)], edge_send.at[0], edge_recv.at[0], next_group)
    start(node_points.at[pl.ds(4, 4)], node_points.at[pl.ds(12, 4)], edge_send.at[1], edge_recv.at[1], previous_group)

    def node_forms(node, carry):
        left, right = forms(doubled(node_points[node]))
        node_left[node] = left
        node_right[node] = right
        return carry

    lax.fori_loop(4, 12, node_forms, 0)

    for pair in range(4):
        rows = slice(pair * RANK, (pair + 1) * RANK)
        below = node_left[4 + 2 * pair : 6 + 2 * pair].reshape(2 * RANK, 256)
        upper_left[rows, :], upper_right[rows, :], _ = picked_forms(nn(chosen(3 + pair), below))
    for quad in range(2):
        rows = slice((4 + quad) * RANK, (5 + quad) * RANK)
        below = slice(2 * quad * RANK, (2 * quad + 2) * RANK)
        upper_left[rows, :], upper_right[rows, :], _ = picked_forms(nn(chosen(7 + quad), upper_left[below, :]))
    _, upper_right[6 * RANK : 7 * RANK, :], top_twice = picked_forms(
        nn(chosen(9), upper_left[4 * RANK : 6 * RANK, :])
    )
    lane = lanes_of((HALF, 128))
    top_points[group] = jnp.where(lane < FEAT, top_twice[:HALF], top_twice[HALF:])
    for step in range(1, TOPS):
        start(top_points.at[group], top_points.at[group], tpts_send.at[step], tpts_recv.at[step], peer(step))

    top_transfer = softmax3(nt(upper_left[4 * RANK : 6 * RANK, :], upper_right[6 * RANK : 7 * RANK, :]))
    for quad in range(2):
        below = slice(2 * quad * RANK, (2 * quad + 2) * RANK)
        transfer = softmax3(nt(upper_left[below, :], upper_right[(4 + quad) * RANK : (5 + quad) * RANK, :]))
        chain = product3(nn, split(transfer), split(top_transfer[quad * RANK : (quad + 1) * RANK]))
        pair_high[below, :], pair_low[below, :] = split(chain)

    def pair_chain(pair, carry):
        rows = pl.ds(pl.multiple_of(pair * RANK, RANK), RANK)
        store = pl.ds(pl.multiple_of(2 * pair * RANK, RANK), 2 * RANK)
        transfer = softmax3(nt(node_left[pl.ds(2 * pair + 4, 2)].reshape(2 * RANK, 256), upper_right[rows, :]))
        chain = product3(nn, split(transfer), (pair_high[rows, :], pair_low[rows, :]))
        chain_high[store, :], chain_low[store, :] = split(chain)
        return carry

    lax.fori_loop(0, 4, pair_chain, 0)

    for step in range(1, GROUP):
        source = 4 + lax.rem(place + GROUP - step, GROUP)
        remote(
            weights_t.at[0], node_values.at[source], gval_send.at[step], gval_recv.at[step], mate(step)
        ).wait_recv()
    start(node_values.at[pl.ds(8, 4)], node_values.at[pl.ds(0, 4)], edge_send.at[2], edge_recv.at[2], next_group)
    start(node_values.at[pl.ds(4, 4)], node_values.at[pl.ds(12, 4)], edge_send.at[3], edge_recv.at[3], previous_group)

    def lift(node, total):
        rows = pl.ds(pl.multiple_of(node * RANK, RANK), RANK)
        return total + thin_product(nn, node_values[4 + node], (chain_high[rows, :], chain_low[rows, :]))

    top_values[group] = lax.fori_loop(0, GROUP, lift, jnp.zeros((SHARE, RANK), F32))
    for step in range(1, TOPS):
        start(top_values.at[group], top_values.at[group], tval_send.at[step], tval_recv.at[step], peer(step))

    def near_tile(leaf, half, position):
        rows = pl.ds(pl.multiple_of(leaf * LEAF + half * 256, 256), 256)
        tile = split(jnp.exp2(nt(leaf_left[rows, :], near_right[position])))
        return rows, product3(nn, tile, (values_high[position], values_low[position]))

    def own_tile(step, carry):
        leaf = step // 2
        rows, value = near_tile(leaf, step % 2, 2 + leaf)
        out[rows, :] = value
        return carry

    lax.fori_loop(0, 4, own_tile, 0)

    for step in range(1, GROUP):
        source = lax.rem(place + GROUP - step, GROUP)
        remote(
            node_lists.at[source], node_lists.at[source], glist_send.at[step], glist_recv.at[step], mate(step)
        ).wait_recv()
    to_scalars = pltpu.make_async_copy(node_lists, list_scalars, local_sem)
    to_scalars.start()
    to_scalars.wait()
    for side, target in ((0, 0), (1, 12)):
        landed = node_points.at[pl.ds(target, 4)]
        remote(landed, landed, edge_send.at[side], edge_recv.at[side], next_group).wait_recv()
    lax.fori_loop(0, 4, node_forms, 0)
    lax.fori_loop(12, 16, node_forms, 0)
    for side, target in ((0, 0), (1, 12)):
        landed = node_values.at[pl.ds(target, 4)]
        remote(landed, landed, edge_send.at[2 + side], edge_recv.at[2 + side], next_group).wait_recv()

    def far_node(node, carry):
        mine_right = node_right[4 + node]
        total = jnp.zeros((SHARE, RANK), F32)
        for slot in range(FAR1):
            entry = list_scalars[node, 0, slot]
            weight = (jnp.minimum(entry, 0) + 1).astype(F32)
            position = jnp.maximum(entry - group * GROUP + 4, 0)
            tile = split(jnp.exp2(nt(node_left[position], mine_right)))
            total = total + weight * thin_product(nn, node_values[position], tile)
        field_out[node] = total
        return carry

    lax.fori_loop(0, GROUP, far_node, 0)

    for step in range(1, TOPS):
        source = lax.rem(group + TOPS - step, TOPS)
        remote(
            top_points.at[source], top_points.at[source], tpts_send.at[step], tpts_recv.at[step], peer(step)
        ).wait_recv()
    for step in range(1, TOPS):
        source = lax.rem(group + TOPS - step, TOPS)
        remote(
            top_values.at[source], top_values.at[source], tval_send.at[step], tval_recv.at[step], peer(step)
        ).wait_recv()
    top_field = jnp.zeros((SHARE, RANK), F32)
    for slot in range(FAR4):
        source = top_far_list[group, slot]
        left, _ = forms(doubled(top_points[source]))
        tile = split(jnp.exp2(nt(left, upper_right[6 * RANK : 7 * RANK, :])))
        top_field = top_field + thin_product(nn, top_values[source], tile)
    for node in range(GROUP):
        rows = slice(node * RANK, (node + 1) * RANK)
        field_out[node] = field_out[node] + thin_product(nt, top_field, (chain_high[rows, :], chain_low[rows, :]))
    for step in range(1, GROUP):
        start(
            field_out.at[lax.rem(place + step, GROUP)],
            field_in.at[place],
            back_send.at[step],
            back_recv.at[step],
            mate(step),
        )
    field_in[place] = field_out[place]

    for side in range(2):
        for part in range(5):
            if part == 0:
                landed = near_points.at[side]
            else:
                landed = near_values.at[side, pl.ds((part - 1) * 256, 256), :]
            remote(landed, landed, near_send.at[side, part], near_recv.at[side, part], right_device).wait_recv()
        packed = near_points[side]
        lane = lanes_of(packed.shape)
        swapped = swap_halves(packed)
        for leaf in range(2):
            twice = jnp.where(lane < FEAT, packed, swapped) if leaf == 0 else jnp.where(lane < FEAT, swapped, packed)
            slot = 4 * side + leaf
            _, near_right[slot] = forms(twice)
            values_high[slot], values_low[slot] = split(near_values[side, leaf * LEAF : (leaf + 1) * LEAF, :])

    def other_tile(step, carry):
        leaf = step // 4
        slot = 1 + (step % 4) // 2
        entry = near_list[leaf, slot]
        position = jnp.maximum(entry - 2 * me + 2, 0)
        weight = (jnp.minimum(entry, 0) + 1).astype(F32)
        rows, value = near_tile(leaf, step % 2, position)
        out[rows, :] = out[rows, :] + weight * value
        return carry

    lax.fori_loop(0, 8, other_tile, 0)

    for step in range(1, GROUP):
        source = lax.rem(place + GROUP - step, GROUP)
        remote(
            field_out.at[0], field_in.at[source], back_send.at[step], back_recv.at[step], mate(step)
        ).wait_recv()
    field = split(field_in[...].reshape(RHS, RANK))

    def finish(step, carry):
        rows = pl.ds(pl.multiple_of(step * 256, 256), 256)
        out[rows, :] = out[rows, :] + product3(nt, (basis_high[rows, :], basis_low[rows, :]), field)
        return carry

    lax.fori_loop(0, 4, finish, 0)
    for copy in started:
        copy.wait_send()


def body(
    points,
    coefficients,
    leaf_skeleton,
    node_skeleton,
    pair_skeleton,
    quad_skeleton,
    top_skeleton,
    near_list,
    far_list,
    top_far_list,
):
    vmem = pl.BlockSpec(memory_space=pltpu.VMEM)
    smem = pl.BlockSpec(memory_space=pltpu.SMEM)
    dma = pltpu.SemaphoreType.DMA
    return pl.pallas_call(
        kernel,
        out_shape=jax.ShapeDtypeStruct((2 * LEAF, RHS), F32),
        in_specs=[smem] * 3 + [vmem] * 7,
        out_specs=vmem,
        scratch_shapes=[
            pltpu.VMEM((LEAF, 128), F32),
            pltpu.VMEM((2, LEAF, 128), F32),
            pltpu.VMEM((2, 2 * LEAF, RHS), F32),
            pltpu.VMEM((16, HALF, 128), F32),
            pltpu.VMEM((16, SHARE, RANK), F32),
            pltpu.VMEM((GROUP, 1, 128), jnp.int32),
            pltpu.SMEM((GROUP, 1, 128), jnp.int32),
            pltpu.VMEM((TOPS, HALF, 128), F32),
            pltpu.VMEM((TOPS, SHARE, RANK), F32),
            pltpu.VMEM((GROUP, SHARE, RANK), F32),
            pltpu.VMEM((GROUP, SHARE, RANK), F32),
            pltpu.VMEM((GROUP, SHARE, RANK), F32),
            pltpu.VMEM((128, RANK), F32),
            pltpu.VMEM((RANK, 128), jnp.int32),
            pltpu.VMEM((2 * LEAF, 256), BF16),
            pltpu.VMEM((6, LEAF, 256), BF16),
            pltpu.VMEM((6, LEAF, RHS), BF16),
            pltpu.VMEM((6, LEAF, RHS), BF16),
            pltpu.VMEM((2 * LEAF, RANK), BF16),
            pltpu.VMEM((2 * LEAF, RANK), BF16),
            pltpu.VMEM((16, RANK, 256), BF16),
            pltpu.VMEM((16, RANK, 256), BF16),
            pltpu.VMEM((7 * RANK, 256), BF16),
            pltpu.VMEM((7 * RANK, 256), BF16),
            pltpu.VMEM((4 * RANK, RANK), BF16),
            pltpu.VMEM((4 * RANK, RANK), BF16),
            pltpu.VMEM((8 * RANK, RANK), BF16),
            pltpu.VMEM((8 * RANK, RANK), BF16),
            dma((2, 5)),
            dma((2, 5)),
            dma((GROUP,)),
            dma((GROUP,)),
            dma((GROUP,)),
            dma((GROUP,)),
            dma((GROUP,)),
            dma((GROUP,)),
            dma((4,)),
            dma((4,)),
            dma((TOPS,)),
            dma((TOPS,)),
            dma((TOPS,)),
            dma((TOPS,)),
            dma((GROUP,)),
            dma((GROUP,)),
            dma,
        ],
        compiler_params=pltpu.CompilerParams(
            collective_id=0, has_side_effects=True, vmem_limit_bytes=56 * 1024 * 1024
        ),
    )(
        near_list,
        far_list,
        top_far_list,
        points,
        coefficients,
        leaf_skeleton,
        node_skeleton,
        pair_skeleton,
        quad_skeleton,
        top_skeleton,
    )


def solution(mesh):
    return jax.shard_map(
        body,
        mesh=mesh,
        in_specs=(
            P("leaf", None),
            P("leaf", None),
            P("leaf", None),
            P("leaf", None),
            P(),
            P(),
            P(),
            P("leaf", None),
            P("leaf", None),
            P(),
        ),
        out_specs=P("leaf", None),
        check_vma=False,
    )
```

profile of v0, /device:TPU:1, one launch (start us, length us, event | category | flops | bytes accessed | tf_op | source)
XLA Modules:
  0.0 85.7 jit_solution(2316388897657425306)
XLA Ops:
  0.0 1.3 %copy.11.top_far_list = s32[16,3]{1,0:T(8,128)} copy(s32[16,3]{0,1:T(4,128)} %param.19) | data formatting | bytes 384 | tf_op args[9]
  1.3 1.9 %copy.12.points = f32[1024,64]{1,0:T(8,128)} copy(f32[1024,64]{0,1:T(8,128)} %param.10) | data formatting | bytes 524288 | tf_op args[0]
  3.3 80.2 %shard_map.100 = f32[1024,256]{1,0:T(8,128)} custom-call(s32[2,3]{1,0:T(2,128)} %near_list.1, s32[1,3]{1,0:T(1,128)} %far_list.1, s32[16,3]{1,0:T(8,128)} %copy.11.top_far_list, f32[1024,64]{1,0:T(8,128)} %copy.12.points, f32[1024,256]{1,0:T(8,128)} %coefficients.1, s32[2,256]{1,0:T(2,128)} %leaf_skeleton.1, s32[1,256]{1,0:T(1,128)} %node_skeleton.1, ...), custom_call_target="tpu_custom_call" | custom-call | tf_op jit(solution)/shard_map/pallas_call | solution.py:507
  83.5 2.3 %copy.14 = f32[1024,256]{1,0:T(8,128)} copy(f32[1024,256]{1,0:T(8,128)} %shard_map.100) | data formatting | bytes 2097152
where the time goes:
time: 86 us; the launch traced here: 85.7 us
  Pallas kernels  80.2 us (93%)
  local copies, waits for them, and re-layouts  5.56 us (6%)
    pallas_call x1, Pallas kernels, body(): pl.pallas_call(kernel, out_shape=jax.ShapeDtypeStruct((2 * LEAF, RHS), F3...  80.2 us
    unnamed x3, local copies, waits for them, and re-layouts  5.56 us

commit v1 on v0

v1 whole, which is shorter than its diff:
```python
import math

import jax
import jax.numpy as jnp
from jax import lax
from jax.experimental import pallas as pl
from jax.experimental.pallas import tpu as pltpu
from jax.sharding import PartitionSpec as P

FEAT = 64
RHS = 256
RANK = 256
LEAF = 512
NEAR = 3
FAR1 = 3
FAR4 = 3
GROUP = 8
TOPS = 16
DEVICES = 128
SHARE = RHS // GROUP
HALF = RANK // 2

MESH = pl.DeviceIdType.MESH
F32 = jnp.float32
BF16 = jnp.bfloat16
SCALE = math.sqrt(2.0 * math.log2(math.e) / FEAT)


def dot(left, right, dims):
    return lax.dot_general(left, right, (dims, ((), ())), preferred_element_type=F32)


def nn(left, right):
    return dot(left, right, ((1,), (0,)))


def nt(left, right):
    return dot(left, right, ((1,), (1,)))


def tn(left, right):
    return dot(left, right, ((0,), (0,)))


def split(values):
    high = values.astype(BF16)
    low = (values - high.astype(F32)).astype(BF16)
    return high, low


def product3(mul, left, right):
    return mul(left[0], right[0]) + (mul(left[0], right[1]) + mul(left[1], right[0]))


def thin_product(mul, left, right):
    rows = left.shape[0]
    high, low = split(left)
    both = mul(jnp.concatenate([high, low], axis=0), right[0])
    return both[:rows] + (both[rows:] + mul(high, right[1]))


def parts(points):
    high = points.astype(BF16).astype(F32)
    low = points - high
    norm = -0.5 * jnp.sum(points * points, axis=0, keepdims=True)
    norm1 = norm.astype(BF16).astype(F32)
    norm2 = (norm - norm1).astype(BF16).astype(F32)
    norm3 = norm - norm1 - norm2
    row = lax.broadcasted_iota(jnp.int32, (16, points.shape[1]), 0)
    norms = jnp.where(row == 0, norm1, jnp.where(row == 1, norm2, jnp.where(row == 2, norm3, 0.0)))
    ones = jnp.where(row < 3, 1.0, 0.0)
    rest = jnp.zeros((32, points.shape[1]), F32)
    return high, low, norms, ones, rest


def right_form(points):
    high, low, norms, ones, rest = parts(points)
    return jnp.concatenate([low, high, high, ones, norms, rest], axis=0).astype(BF16)


def left_of(right):
    return jnp.concatenate(
        [right[64:128], right[0:64], right[128:192], right[208:224], right[192:208], right[224:256]], axis=0
    )


def exponents(left_points, right_points):
    return tn(left_of(left_points), right_points)


def pick(candidates, table_row):
    spread = lax.broadcasted_iota(jnp.int32, (2 * RANK, RANK), 0)
    chosen = jnp.where(spread == table_row, 1.0, 0.0).astype(BF16)
    picked = nn(candidates, chosen)
    return picked.astype(BF16), picked[0:64] + picked[64:128]


def softmax3(exponent):
    top = jnp.max(exponent, axis=0, keepdims=True)
    weights = jnp.exp2(3.0 * (exponent - top))
    return weights / jnp.sum(weights, axis=0, keepdims=True)


def kernel(
    near_list,
    far_list,
    top_far_list,
    points,
    coefficients,
    leaf_skeleton,
    node_skeleton,
    pair_skeleton,
    quad_skeleton,
    top_skeleton,
    out,
    near_points,
    near_values,
    node_points,
    node_values,
    node_lists,
    list_scalars,
    top_points,
    top_values,
    field_out,
    field_in,
    weights_t,
    leaf_left,
    near_right,
    values_high,
    values_low,
    basis_t_high,
    basis_t_low,
    basis_high,
    basis_low,
    node_right,
    upper_right,
    chain_high,
    chain_low,
    near_send,
    near_recv,
    gpts_send,
    gpts_recv,
    glist_send,
    glist_recv,
    gval_send,
    gval_recv,
    edge_send,
    edge_recv,
    tpts_send,
    tpts_recv,
    tval_send,
    tval_recv,
    back_send,
    back_recv,
    local_sem,
):
    me = lax.axis_index("leaf")
    place = lax.rem(me, GROUP)
    group = me // GROUP
    right_device = lax.rem(me + 1, DEVICES)
    left_device = lax.rem(me + DEVICES - 1, DEVICES)
    next_group = lax.rem(group + 1, TOPS) * GROUP + place
    previous_group = lax.rem(group + TOPS - 1, TOPS) * GROUP + place

    core = lax.rem(place, 2)
    sibling_place = place + 1 - 2 * core
    sibling = group * GROUP + sibling_place

    def mate(step):
        return group * GROUP + lax.rem(place + step, GROUP)

    def peer(step):
        return lax.rem(group + step, TOPS) * GROUP + place

    barrier = pltpu.get_barrier_semaphore()
    partners = [right_device, left_device]
    partners += [mate(step) for step in range(1, GROUP)]
    partners += [peer(step) for step in range(1, TOPS)]
    for partner in partners:
        pl.semaphore_signal(barrier, inc=1, device_id=(partner,), device_id_type=MESH)

    def remote(source, target, send, recv, device):
        return pltpu.make_async_remote_copy(
            src_ref=source, dst_ref=target, send_sem=send, recv_sem=recv, device_id=(device,), device_id_type=MESH
        )

    started = []

    def start(*args):
        copy = remote(*args)
        copy.start()
        started.append(copy)

    high, low, norms, ones, rest = parts(points[...] * SCALE)
    right_rows = jnp.concatenate([low, high, high, ones, norms, rest], axis=0).astype(BF16)
    leaf_picks = []
    for leaf in range(2):
        right = right_rows[:, leaf * LEAF : (leaf + 1) * LEAF]
        near_right[2 + leaf] = right
        leaf_picks.append(pick(right, leaf_skeleton[leaf : leaf + 1, :])[0])
    picks = jnp.concatenate(leaf_picks, axis=1)
    node_pick, node_pick_points = pick(picks, node_skeleton[...])
    node_points[4 + place] = node_pick_points
    lane_row = lax.broadcasted_iota(jnp.int32, (1, 128), 1)
    node_lists[place] = jnp.where(
        lane_row == 0, far_list[0, 0], jnp.where(lane_row == 1, far_list[0, 1], far_list[0, 2])
    )
    pl.semaphore_wait(barrier, len(partners))
    mine = node_points.at[4 + place]
    for step in (2, 4, 6):
        start(mine, mine, gpts_send.at[step], gpts_recv.at[step], mate(step))
    start(mine, mine, gpts_send.at[0], gpts_recv.at[0], sibling)

    transfer = split(softmax3(exponents(node_pick, picks)))
    for leaf in range(2):
        rows = slice(leaf * LEAF, (leaf + 1) * LEAF)
        half = slice(leaf * RANK, (leaf + 1) * RANK)
        basis = softmax3(exponents(leaf_picks[leaf], near_right[2 + leaf]))
        basis_t = product3(nn, (transfer[0][:, half], transfer[1][:, half]), split(basis))
        basis_t_high[:, rows], basis_t_low[:, rows] = split(basis_t)
        values_high[2 + leaf], values_low[2 + leaf] = split(coefficients[rows, :])
    weights = product3(
        nn,
        (basis_t_high[...], basis_t_low[...]),
        (values_high[2:4].reshape(2 * LEAF, RHS), values_low[2:4].reshape(2 * LEAF, RHS)),
    )
    weights_t[...] = jnp.transpose(weights).reshape(GROUP, SHARE, RANK)
    for step in range(1, GROUP):
        start(
            weights_t.at[lax.rem(place + step, GROUP)],
            node_values.at[4 + place],
            gval_send.at[step],
            gval_recv.at[step],
            mate(step),
        )
    node_values[4 + place] = weights_t[place]
    for step in range(1, GROUP):
        start(node_lists.at[place], node_lists.at[place], glist_send.at[step], glist_recv.at[step], mate(step))

    for side, device in ((0, right_device), (1, left_device)):
        start(points, near_points.at[side], near_send.at[side, 0], near_recv.at[side, 0], device)
        for part in range(4):
            rows = pl.ds(part * 256, 256)
            start(
                coefficients.at[rows, :],
                near_values.at[side, rows, :],
                near_send.at[side, part + 1],
                near_recv.at[side, part + 1],
                device,
            )

    def near_tile(leaf, half, position):
        rows = pl.ds(pl.multiple_of(leaf * LEAF + half * 256, 256), 256)
        tile = split(jnp.exp2(nn(leaf_left[rows, :], near_right[position])))
        return rows, product3(nn, tile, (values_high[position], values_low[position]))

    left_rows = jnp.concatenate([high, low, high, norms, ones, rest], axis=0)
    for leaf in range(2):
        rows = slice(leaf * LEAF, (leaf + 1) * LEAF)
        leaf_left[rows, :] = jnp.transpose(left_rows[:, rows]).astype(BF16)
        for half in range(2):
            tile_rows, value = near_tile(leaf, half, 2 + leaf)
            out[tile_rows, :] = value

    for step in (2, 4, 6):
        landed = node_points.at[4 + lax.rem(place + GROUP - step, GROUP)]
        remote(landed, landed, gpts_send.at[step], gpts_recv.at[step], sibling).wait_recv()
        start(landed, landed, gpts_send.at[1 + step], gpts_recv.at[1 + step], sibling)
    for leaf in range(2):
        rows = slice(leaf * LEAF, (leaf + 1) * LEAF)
        basis_high[rows, :] = jnp.transpose(basis_t_high[:, rows].astype(F32)).astype(BF16)
        basis_low[rows, :] = jnp.transpose(basis_t_low[:, rows].astype(F32)).astype(BF16)
    landed = node_points.at[4 + sibling_place]
    remote(landed, landed, gpts_send.at[0], gpts_recv.at[0], sibling).wait_recv()
    for step in (2, 4, 6):
        landed = node_points.at[4 + lax.rem(sibling_place + GROUP - step, GROUP)]
        remote(landed, landed, gpts_send.at[1 + step], gpts_recv.at[1 + step], sibling).wait_recv()
    for node in range(4, 12):
        node_right[node] = right_form(node_points[node])

    pair_candidates = [
        jnp.concatenate([node_right[4 + 2 * pair], node_right[5 + 2 * pair]], axis=1) for pair in range(4)
    ]
    for pair in range(4):
        upper_right[pair] = pick(pair_candidates[pair], pair_skeleton[pl.ds(group * 4 + pair, 1), :])[0]
    quad_candidates = [
        jnp.concatenate([upper_right[2 * quad], upper_right[2 * quad + 1]], axis=1) for quad in range(2)
    ]
    for quad in range(2):
        upper_right[4 + quad] = pick(quad_candidates[quad], quad_skeleton[pl.ds(group * 2 + quad, 1), :])[0]
    top_candidates = jnp.concatenate([upper_right[4], upper_right[5]], axis=1)
    top_right, top_picked = pick(top_candidates, top_skeleton[pl.ds(group, 1), :])
    upper_right[6] = top_right
    top_points[core, group] = jnp.where(core == 0, top_picked[0:32], top_picked[32:64])
    share = top_points.at[core, group]
    for step in range(1, TOPS):
        start(share, share, tpts_send.at[step], tpts_recv.at[step], peer(step))
    for side, source, target, device in ((0, 8, 0, next_group), (1, 4, 12, previous_group)):
        start(
            node_points.at[pl.ds(source + 2 * core, 2)],
            node_points.at[pl.ds(target + 2 * core, 2)],
            edge_send.at[side],
            edge_recv.at[side],
            device,
        )

    top_transfer = split(softmax3(exponents(upper_right[6], top_candidates)))
    for quad in range(2):
        half = slice(quad * RANK, (quad + 1) * RANK)
        transfer = split(softmax3(exponents(upper_right[4 + quad], quad_candidates[quad])))
        upper = split(product3(nn, (top_transfer[0][:, half], top_transfer[1][:, half]), transfer))
        for side in range(2):
            pair = 2 * quad + side
            half = slice(side * RANK, (side + 1) * RANK)
            transfer = split(softmax3(exponents(upper_right[pair], pair_candidates[pair])))
            chain = split(product3(nn, (upper[0][:, half], upper[1][:, half]), transfer))
            for child in range(2):
                columns = slice(child * RANK, (child + 1) * RANK)
                chain_high[2 * pair + child] = chain[0][:, columns]
                chain_low[2 * pair + child] = chain[1][:, columns]

    for step in range(1, GROUP):
        source = 4 + lax.rem(place + GROUP - step, GROUP)
        remote(
            weights_t.at[0], node_values.at[source], gval_send.at[step], gval_recv.at[step], mate(step)
        ).wait_recv()
    start(node_values.at[pl.ds(8, 4)], node_values.at[pl.ds(0, 4)], edge_send.at[2], edge_recv.at[2], next_group)
    start(node_values.at[pl.ds(4, 4)], node_values.at[pl.ds(12, 4)], edge_send.at[3], edge_recv.at[3], previous_group)
    total = jnp.zeros((SHARE, RANK), F32)
    for node in range(GROUP):
        total = total + thin_product(nt, node_values[4 + node], (chain_high[node], chain_low[node]))
    top_values[group] = total
    for step in range(1, TOPS):
        start(top_values.at[group], top_values.at[group], tval_send.at[step], tval_recv.at[step], peer(step))

    for side, target in ((0, 0), (1, 12)):
        landed = node_points.at[pl.ds(target + 2 * core, 2)]
        remote(landed, landed, edge_send.at[side], edge_recv.at[side], sibling).wait_recv()
        start(landed, landed, edge_send.at[4 + side], edge_recv.at[4 + side], sibling)
    for step in range(1, GROUP):
        source = lax.rem(place + GROUP - step, GROUP)
        remote(
            node_lists.at[source], node_lists.at[source], glist_send.at[step], glist_recv.at[step], mate(step)
        ).wait_recv()
    to_scalars = pltpu.make_async_copy(node_lists, list_scalars, local_sem)
    to_scalars.start()
    to_scalars.wait()
    for side, target in ((0, 0), (1, 12)):
        landed = node_points.at[pl.ds(target + 2 - 2 * core, 2)]
        remote(landed, landed, edge_send.at[4 + side], edge_recv.at[4 + side], sibling).wait_recv()
    for node in (0, 1, 2, 3, 12, 13, 14, 15):
        node_right[node] = right_form(node_points[node])
    for side, target in ((0, 0), (1, 12)):
        landed = node_values.at[pl.ds(target, 4)]
        remote(landed, landed, edge_send.at[2 + side], edge_recv.at[2 + side], sibling).wait_recv()

    def far_node(node, carry):
        mine_right = node_right[4 + node]
        total = jnp.zeros((SHARE, RANK), F32)
        for slot in range(FAR1):
            entry = list_scalars[node, 0, slot]
            weight = (jnp.minimum(entry, 0) + 1).astype(F32)
            position = jnp.maximum(entry - group * GROUP + 4, 0)
            tile = split(jnp.exp2(exponents(node_right[position], mine_right)))
            total = total + weight * thin_product(nn, node_values[position], tile)
        field_out[node] = total
        return carry

    lax.fori_loop(0, GROUP // 2, far_node, 0, unroll=2)
    for step in range(1, TOPS):
        landed = top_points.at[core, lax.rem(group + TOPS - step, TOPS)]
        remote(landed, landed, tpts_send.at[step], tpts_recv.at[step], sibling).wait_recv()
    start(top_points.at[core], top_points.at[core], tpts_send.at[0], tpts_recv.at[0], sibling)
    lax.fori_loop(GROUP // 2, GROUP, far_node, 0, unroll=2)

    landed = top_points.at[1 - core]
    remote(landed, landed, tpts_send.at[0], tpts_recv.at[0], sibling).wait_recv()
    tiles = []
    for slot in range(FAR4):
        source = top_far_list[slot, group]
        tiles.append(split(jnp.exp2(exponents(right_form(top_points[:, source].reshape(FEAT, RANK)), upper_right[6]))))
    for step in range(1, TOPS):
        source = lax.rem(group + TOPS - step, TOPS)
        remote(
            top_values.at[source], top_values.at[source], tval_send.at[step], tval_recv.at[step], peer(step)
        ).wait_recv()
    top_field = jnp.zeros((SHARE, RANK), F32)
    for slot in range(FAR4):
        source = top_far_list[slot, group]
        top_field = top_field + thin_product(nn, top_values[source], tiles[slot])
    for node in range(GROUP):
        field_out[node] = field_out[node] + thin_product(nn, top_field, (chain_high[node], chain_low[node]))
    for step in range(1, GROUP):
        start(
            field_out.at[lax.rem(place + step, GROUP)],
            field_in.at[place],
            back_send.at[step],
            back_recv.at[step],
            mate(step),
        )
    field_in[place] = field_out[place]

    for side in range(2):
        for part in range(5):
            if part == 0:
                landed = near_points.at[side]
            else:
                landed = near_values.at[side, pl.ds((part - 1) * 256, 256), :]
            remote(landed, landed, near_send.at[side, part], near_recv.at[side, part], right_device).wait_recv()
        for leaf in range(2):
            slot = 4 * side + leaf
            rows = slice(leaf * LEAF, (leaf + 1) * LEAF)
            near_right[slot] = right_form(near_points[side, :, rows] * SCALE)
            values_high[slot], values_low[slot] = split(near_values[side, rows, :])

    def other_tile(step, carry):
        leaf = step // 2
        entry = near_list[leaf, 1 + step % 2]
        position = jnp.maximum(entry - 2 * me + 2, 0)
        weight = (jnp.minimum(entry, 0) + 1).astype(F32)
        for half in range(2):
            rows, value = near_tile(leaf, half, position)
            out[rows, :] = out[rows, :] + weight * value
        return carry

    lax.fori_loop(0, 4, other_tile, 0)

    for step in range(1, GROUP):
        source = lax.rem(place + GROUP - step, GROUP)
        remote(
            field_out.at[0], field_in.at[source], back_send.at[step], back_recv.at[step], mate(step)
        ).wait_recv()
    field = split(jnp.transpose(field_in[...].reshape(RHS, RANK)))
    for quarter in range(4):
        rows = slice(quarter * 256, (quarter + 1) * 256)
        out[rows, :] = out[rows, :] + product3(nn, (basis_high[rows, :], basis_low[rows, :]), field)
    for copy in started:
        copy.wait_send()


def body(
    points,
    coefficients,
    leaf_skeleton,
    node_skeleton,
    pair_skeleton,
    quad_skeleton,
    top_skeleton,
    near_list,
    far_list,
    top_far_list,
):
    vmem = pl.BlockSpec(memory_space=pltpu.VMEM)
    smem = pl.BlockSpec(memory_space=pltpu.SMEM)
    dma = pltpu.SemaphoreType.DMA
    return pl.pallas_call(
        kernel,
        out_shape=jax.ShapeDtypeStruct((2 * LEAF, RHS), F32),
        in_specs=[smem] * 3 + [vmem] * 7,
        out_specs=vmem,
        scratch_shapes=[
            pltpu.VMEM((2, FEAT, 2 * LEAF), F32),
            pltpu.VMEM((2, 2 * LEAF, RHS), F32),
            pltpu.VMEM((16, FEAT, RANK), F32),
            pltpu.VMEM((16, SHARE, RANK), F32),
            pltpu.VMEM((GROUP, 1, 128), jnp.int32),
            pltpu.SMEM((GROUP, 1, 128), jnp.int32),
            pltpu.VMEM((2, TOPS, FEAT // 2, RANK), F32),
            pltpu.VMEM((TOPS, SHARE, RANK), F32),
            pltpu.VMEM((GROUP, SHARE, RANK), F32),
            pltpu.VMEM((GROUP, SHARE, RANK), F32),
            pltpu.VMEM((GROUP, SHARE, RANK), F32),
            pltpu.VMEM((2 * LEAF, 256), BF16),
            pltpu.VMEM((6, 256, LEAF), BF16),
            pltpu.VMEM((6, LEAF, RHS), BF16),
            pltpu.VMEM((6, LEAF, RHS), BF16),
            pltpu.VMEM((RANK, 2 * LEAF), BF16),
            pltpu.VMEM((RANK, 2 * LEAF), BF16),
            pltpu.VMEM((2 * LEAF, RANK), BF16),
            pltpu.VMEM((2 * LEAF, RANK), BF16),
            pltpu.VMEM((16, 256, RANK), BF16),
            pltpu.VMEM((7, 256, RANK), BF16),
            pltpu.VMEM((GROUP, RANK, RANK), BF16),
            pltpu.VMEM((GROUP, RANK, RANK), BF16),
            dma((2, 5)),
            dma((2, 5)),
            dma((GROUP,)),
            dma((GROUP,)),
            dma((GROUP,)),
            dma((GROUP,)),
            dma((GROUP,)),
            dma((GROUP,)),
            dma((6,)),
            dma((6,)),
            dma((TOPS,)),
            dma((TOPS,)),
            dma((TOPS,)),
            dma((TOPS,)),
            dma((GROUP,)),
            dma((GROUP,)),
            dma,
        ],
        compiler_params=pltpu.CompilerParams(
            collective_id=0, has_side_effects=True, vmem_limit_bytes=56 * 1024 * 1024
        ),
    )(
        near_list,
        far_list,
        top_far_list.T,
        points.T,
        coefficients,
        leaf_skeleton,
        node_skeleton,
        pair_skeleton,
        quad_skeleton,
        top_skeleton,
    )


def solution(mesh):
    return jax.shard_map(
        body,
        mesh=mesh,
        in_specs=(
            P("leaf", None),
            P("leaf", None),
            P("leaf", None),
            P("leaf", None),
            P(),
            P(),
            P(),
            P("leaf", None),
            P("leaf", None),
            P(),
        ),
        out_specs=P("leaf", None),
        check_vma=False,
    )
```

time: 86 us -> 60.9 us (0.71)
  Pallas kernels: 80.2 us -> 58.4 us
  local copies, waits for them, and re-layouts: 5.56 us -> 2.26 us
    pallas_call x1, Pallas kernels: 80.2 us -> 58.4 us  [body(): pl.pallas_call(kernel, out_shape=jax.ShapeDtypeStruct((2 * LEAF, RHS), F3...]
    unnamed x3 -> x1, local copies, waits for them, and re-layouts: 5.56 us -> 2.26 us
where the time goes in v1:
time: 60.9 us; the launch traced here: 60.7 us
  Pallas kernels  58.4 us (96%)
  local copies, waits for them, and re-layouts  2.26 us (4%)
    pallas_call x1, Pallas kernels, body(): pl.pallas_call(kernel, out_shape=jax.ShapeDtypeStruct((2 * LEAF, RHS), F3...  58.4 us
    unnamed x1, local copies, waits for them, and re-layouts  2.26 us

profile of v1, /device:TPU:1, one launch (start us, length us, event | category | flops | bytes accessed | tf_op | source)
XLA Modules:
  0.0 60.7 jit_solution(14991842586243457654)
XLA Ops:
  0.0 58.4 %shard_map.100 = f32[1024,256]{1,0:T(8,128)} custom-call(s32[2,3]{1,0:T(2,128)} %near_list.1, s32[1,3]{1,0:T(1,128)} %far_list.1, s32[3,16]{1,0:T(4,128)} %bitcast.3, f32[64,1024]{1,0:T(8,128)} %bitcast.2, f32[1024,256]{1,0:T(8,128)} %coefficients.1, s32[2,256]{1,0:T(2,128)} %leaf_skeleton.1, s32[1,256]{1,0:T(1,128)} %node_skeleton.1, ...), custom_call_target="tpu_custom_call" | custom-call | tf_op jit(solution)/shard_map/pallas_call | solution.py:456
  58.4 2.3 %copy.12 = f32[1024,256]{1,0:T(8,128)} copy(f32[1024,256]{1,0:T(8,128)} %shard_map.100) | data formatting | bytes 2097152

commit v2 on v1

--- a/solution.py
+++ b/solution.py
@@ -16,7 +16,6 @@
 FAR4 = 3
 GROUP = 8
 TOPS = 16
-DEVICES = 128
 SHARE = RHS // GROUP
 HALF = RANK // 2
 
@@ -138,6 +137,7 @@
     chain_low,
     near_send,
     near_recv,
+    relay_send,
     gpts_send,
     gpts_recv,
     glist_send,
@@ -157,8 +157,6 @@
     me = lax.axis_index("leaf")
     place = lax.rem(me, GROUP)
     group = me // GROUP
-    right_device = lax.rem(me + 1, DEVICES)
-    left_device = lax.rem(me + DEVICES - 1, DEVICES)
     next_group = lax.rem(group + 1, TOPS) * GROUP + place
     previous_group = lax.rem(group + TOPS - 1, TOPS) * GROUP + place
 
@@ -173,8 +171,7 @@
         return lax.rem(group + step, TOPS) * GROUP + place
 
     barrier = pltpu.get_barrier_semaphore()
-    partners = [right_device, left_device]
-    partners += [mate(step) for step in range(1, GROUP)]
+    partners = [mate(step) for step in range(1, GROUP)]
     partners += [peer(step) for step in range(1, TOPS)]
     for partner in partners:
         pl.semaphore_signal(barrier, inc=1, device_id=(partner,), device_id_type=MESH)
@@ -237,17 +234,36 @@
     for step in range(1, GROUP):
         start(node_lists.at[place], node_lists.at[place], glist_send.at[step], glist_recv.at[step], mate(step))
 
-    for side, device in ((0, right_device), (1, left_device)):
-        start(points, near_points.at[side], near_send.at[side, 0], near_recv.at[side, 0], device)
-        for part in range(4):
-            rows = pl.ds(part * 256, 256)
-            start(
-                coefficients.at[rows, :],
-                near_values.at[side, rows, :],
-                near_send.at[side, part + 1],
-                near_recv.at[side, part + 1],
-                device,
+    def near_refs(slot, half):
+        columns = pl.ds(half * LEAF, LEAF)
+        return near_points.at[slot, :, columns], near_values.at[slot, columns, :]
+
+    def relay(slot, half, target, device):
+        for kind, landed in enumerate(near_refs(slot, half)):
+            part = 2 * half + kind
+            send = relay_send.at[target, kind]
+            yield (
+                (landed, landed, send, near_recv.at[slot, part], device),
+                (landed, near_refs(target, half)[kind], send, near_recv.at[target, part], device),
             )
+
+    def relays():
+        at_end = [relay(2, 0, 0, mate(1)), relay(3, 1, 1, previous_group)]
+        at_start = [relay(2, 1, 0, next_group), relay(3, 0, 1, mate(GROUP - 1))]
+        return ((place == GROUP - 1, at_end), (place == 0, at_start))
+
+    last = place // (GROUP - 1)
+    first = (GROUP - 1 - place) // (GROUP - 1)
+    for half in range(2):
+        columns = pl.ds(half * LEAF, LEAF)
+        for side, edge, inner, outer in ((0, last, mate(1), next_group), (1, first, mate(GROUP - 1), previous_group)):
+            slot = side + 2 * edge
+            device = (1 - edge) * inner + edge * (outer if half == 0 else inner)
+            for kind, source in enumerate((points.at[:, columns], coefficients.at[columns, :])):
+                part = 2 * half + kind
+                start(
+                    source, near_refs(slot, half)[kind], near_send.at[side, part], near_recv.at[slot, part], device
+                )
 
     def near_tile(leaf, half, position):
         rows = pl.ds(pl.multiple_of(leaf * LEAF + half * 256, 256), 256)
@@ -332,6 +348,15 @@
     top_values[group] = total
     for step in range(1, TOPS):
         start(top_values.at[group], top_values.at[group], tval_send.at[step], tval_recv.at[step], peer(step))
+
+    for here, paths in relays():
+
+        @pl.when(here)
+        def _():
+            for path in paths:
+                for arrived, copy in path:
+                    remote(*arrived).wait_recv()
+                    remote(*copy).start()
 
     for side, target in ((0, 0), (1, 12)):
         landed = node_points.at[pl.ds(target + 2 * core, 2)]
@@ -401,12 +426,10 @@
     field_in[place] = field_out[place]
 
     for side in range(2):
-        for part in range(5):
-            if part == 0:
-                landed = near_points.at[side]
-            else:
-                landed = near_values.at[side, pl.ds((part - 1) * 256, 256), :]
-            remote(landed, landed, near_send.at[side, part], near_recv.at[side, part], right_device).wait_recv()
+        for half in range(2):
+            for kind, landed in enumerate(near_refs(side, half)):
+                part = 2 * half + kind
+                remote(landed, landed, near_send.at[side, part], near_recv.at[side, part], sibling).wait_recv()
         for leaf in range(2):
             slot = 4 * side + leaf
             rows = slice(leaf * LEAF, (leaf + 1) * LEAF)
@@ -436,6 +459,13 @@
         out[rows, :] = out[rows, :] + product3(nn, (basis_high[rows, :], basis_low[rows, :]), field)
     for copy in started:
         copy.wait_send()
+    for here, paths in relays():
+
+        @pl.when(here)
+        def _():
+            for path in paths:
+                for _, copy in path:
+                    remote(*copy).wait_send()
 
 
 def body(
@@ -459,8 +489,8 @@
         in_specs=[smem] * 3 + [vmem] * 7,
         out_specs=vmem,
         scratch_shapes=[
-            pltpu.VMEM((2, FEAT, 2 * LEAF), F32),
-            pltpu.VMEM((2, 2 * LEAF, RHS), F32),
+            pltpu.VMEM((4, FEAT, 2 * LEAF), F32),
+            pltpu.VMEM((4, 2 * LEAF, RHS), F32),
             pltpu.VMEM((16, FEAT, RANK), F32),
             pltpu.VMEM((16, SHARE, RANK), F32),
             pltpu.VMEM((GROUP, 1, 128), jnp.int32),
@@ -482,8 +512,9 @@
             pltpu.VMEM((7, 256, RANK), BF16),
             pltpu.VMEM((GROUP, RANK, RANK), BF16),
             pltpu.VMEM((GROUP, RANK, RANK), BF16),
-            dma((2, 5)),
-            dma((2, 5)),
+            dma((2, 4)),
+            dma((4, 4)),
+            dma((2, 2)),
             dma((GROUP,)),
             dma((GROUP,)),
             dma((GROUP,)),

time: 60.9 us -> 55.2 us (0.906)
  the two profiles are of different devices: /device:TPU:1 before, /device:TPU:2 now
where the time goes in v2:
time: 55.2 us; the launch traced here: 55.1 us
  Pallas kernels  52.8 us (96%)
  local copies, waits for them, and re-layouts  2.26 us (4%)
    pallas_call x1, Pallas kernels, body(): pl.pallas_call(kernel, out_shape=jax.ShapeDtypeStruct((2 * LEAF, RHS), F3...  52.8 us
    unnamed x1, local copies, waits for them, and re-layouts  2.26 us

profile of v2, /device:TPU:2, one launch (start us, length us, event | category | flops | bytes accessed | tf_op | source)
XLA Modules:
  0.0 55.1 jit_solution(13714237786267656789)
XLA Ops:
  0.0 52.8 %shard_map.100 = f32[1024,256]{1,0:T(8,128)} custom-call(s32[2,3]{1,0:T(2,128)} %near_list.1, s32[1,3]{1,0:T(1,128)} %far_list.1, s32[3,16]{1,0:T(4,128)} %bitcast.3, f32[64,1024]{1,0:T(8,128)} %bitcast.2, f32[1024,256]{1,0:T(8,128)} %coefficients.1, s32[2,256]{1,0:T(2,128)} %leaf_skeleton.1, s32[1,256]{1,0:T(1,128)} %node_skeleton.1, ...), custom_call_target="tpu_custom_call" | custom-call | tf_op jit(solution)/shard_map/pallas_call | solution.py:486
  52.8 2.3 %copy.12 = f32[1024,256]{1,0:T(8,128)} copy(f32[1024,256]{1,0:T(8,128)} %shard_map.100) | data formatting | bytes 2097152

commit v3 on v2

--- a/solution.py
+++ b/solution.py
@@ -120,6 +120,11 @@
     list_scalars,
     top_points,
     top_values,
+    top_share,
+    top_out,
+    top_in,
+    top_high,
+    top_low,
     field_out,
     field_in,
     weights_t,
@@ -150,6 +155,8 @@
     tpts_recv,
     tval_send,
     tval_recv,
+    tout_send,
+    tout_recv,
     back_send,
     back_recv,
     local_sem,
@@ -167,6 +174,12 @@
     def mate(step):
         return group * GROUP + lax.rem(place + step, GROUP)
 
+    quarter = lax.rem(group, 4)
+    ring_first = group - quarter
+
+    def ring(step):
+        return (ring_first + lax.rem(quarter + step, 4)) * GROUP + place
+
     def peer(step):
         return lax.rem(group + step, TOPS) * GROUP + place
 
@@ -187,6 +200,54 @@
         copy = remote(*args)
         copy.start()
         started.append(copy)
+
+    def near_refs(slot, half):
+        columns = pl.ds(half * LEAF, LEAF)
+        return near_points.at[slot, :, columns], near_values.at[slot, columns, :]
+
+    def relay(slot, half, target, device):
+        for kind, landed in enumerate(near_refs(slot, half)):
+            part = 2 * half + kind
+            send = relay_send.at[target, kind]
+            yield (
+                (landed, landed, send, near_recv.at[slot, part], device),
+                (landed, near_refs(target, half)[kind], send, near_recv.at[target, part], device),
+            )
+
+    def relays(half):
+        if half == 0:
+            at_end, at_start = relay(2, 0, 0, mate(1)), relay(3, 0, 1, mate(GROUP - 1))
+        else:
+            at_end, at_start = relay(3, 1, 1, previous_group), relay(2, 1, 0, next_group)
+        return ((place == GROUP - 1, at_end), (place == 0, at_start))
+
+    def pass_on(half):
+        for here, path in relays(half):
+
+            @pl.when(here)
+            def _():
+                for arrived, copy in path:
+                    remote(*arrived).wait_recv()
+                    remote(*copy).start()
+
+    last = place // (GROUP - 1)
+    first = (GROUP - 1 - place) // (GROUP - 1)
+    def near_sends(half, at_edge):
+        columns = pl.ds(half * LEAF, LEAF)
+        for side, edge, inner, outer in ((0, last, mate(1), next_group), (1, first, mate(GROUP - 1), previous_group)):
+
+            @pl.when(edge == at_edge)
+            def _():
+                slot = side + 2 * at_edge
+                device = outer if at_edge and half == 0 else inner
+                for kind, source in enumerate((points.at[:, columns], coefficients.at[columns, :])):
+                    part = 2 * half + kind
+                    remote(
+                        source, near_refs(slot, half)[kind], near_send.at[side, part], near_recv.at[slot, part], device
+                    ).start()
+
+    pl.semaphore_wait(barrier, len(partners))
+    near_sends(0, 1)
 
     high, low, norms, ones, rest = parts(points[...] * SCALE)
     right_rows = jnp.concatenate([low, high, high, ones, norms, rest], axis=0).astype(BF16)
@@ -202,7 +263,6 @@
     node_lists[place] = jnp.where(
         lane_row == 0, far_list[0, 0], jnp.where(lane_row == 1, far_list[0, 1], far_list[0, 2])
     )
-    pl.semaphore_wait(barrier, len(partners))
     mine = node_points.at[4 + place]
     for step in (2, 4, 6):
         start(mine, mine, gpts_send.at[step], gpts_recv.at[step], mate(step))
@@ -234,63 +294,32 @@
     for step in range(1, GROUP):
         start(node_lists.at[place], node_lists.at[place], glist_send.at[step], glist_recv.at[step], mate(step))
 
-    def near_refs(slot, half):
-        columns = pl.ds(half * LEAF, LEAF)
-        return near_points.at[slot, :, columns], near_values.at[slot, columns, :]
-
-    def relay(slot, half, target, device):
-        for kind, landed in enumerate(near_refs(slot, half)):
-            part = 2 * half + kind
-            send = relay_send.at[target, kind]
-            yield (
-                (landed, landed, send, near_recv.at[slot, part], device),
-                (landed, near_refs(target, half)[kind], send, near_recv.at[target, part], device),
-            )
-
-    def relays():
-        at_end = [relay(2, 0, 0, mate(1)), relay(3, 1, 1, previous_group)]
-        at_start = [relay(2, 1, 0, next_group), relay(3, 0, 1, mate(GROUP - 1))]
-        return ((place == GROUP - 1, at_end), (place == 0, at_start))
-
-    last = place // (GROUP - 1)
-    first = (GROUP - 1 - place) // (GROUP - 1)
-    for half in range(2):
-        columns = pl.ds(half * LEAF, LEAF)
-        for side, edge, inner, outer in ((0, last, mate(1), next_group), (1, first, mate(GROUP - 1), previous_group)):
-            slot = side + 2 * edge
-            device = (1 - edge) * inner + edge * (outer if half == 0 else inner)
-            for kind, source in enumerate((points.at[:, columns], coefficients.at[columns, :])):
-                part = 2 * half + kind
-                start(
-                    source, near_refs(slot, half)[kind], near_send.at[side, part], near_recv.at[slot, part], device
-                )
+    near_sends(1, 1)
+    near_sends(0, 0)
+    near_sends(1, 0)
 
     def near_tile(leaf, half, position):
         rows = pl.ds(pl.multiple_of(leaf * LEAF + half * 256, 256), 256)
         tile = split(jnp.exp2(nn(leaf_left[rows, :], near_right[position])))
         return rows, product3(nn, tile, (values_high[position], values_low[position]))
 
-    left_rows = jnp.concatenate([high, low, high, norms, ones, rest], axis=0)
-    for leaf in range(2):
-        rows = slice(leaf * LEAF, (leaf + 1) * LEAF)
-        leaf_left[rows, :] = jnp.transpose(left_rows[:, rows]).astype(BF16)
-        for half in range(2):
-            tile_rows, value = near_tile(leaf, half, 2 + leaf)
-            out[tile_rows, :] = value
-
     for step in (2, 4, 6):
         landed = node_points.at[4 + lax.rem(place + GROUP - step, GROUP)]
         remote(landed, landed, gpts_send.at[step], gpts_recv.at[step], sibling).wait_recv()
         start(landed, landed, gpts_send.at[1 + step], gpts_recv.at[1 + step], sibling)
-    for leaf in range(2):
-        rows = slice(leaf * LEAF, (leaf + 1) * LEAF)
-        basis_high[rows, :] = jnp.transpose(basis_t_high[:, rows].astype(F32)).astype(BF16)
-        basis_low[rows, :] = jnp.transpose(basis_t_low[:, rows].astype(F32)).astype(BF16)
     landed = node_points.at[4 + sibling_place]
     remote(landed, landed, gpts_send.at[0], gpts_recv.at[0], sibling).wait_recv()
     for step in (2, 4, 6):
         landed = node_points.at[4 + lax.rem(sibling_place + GROUP - step, GROUP)]
         remote(landed, landed, gpts_send.at[1 + step], gpts_recv.at[1 + step], sibling).wait_recv()
+    for side, source, target, device in ((0, 8, 0, next_group), (1, 4, 12, previous_group)):
+        start(
+            node_points.at[pl.ds(source + 2 * core, 2)],
+            node_points.at[pl.ds(target + 2 * core, 2)],
+            edge_send.at[side],
+            edge_recv.at[side],
+            device,
+        )
     for node in range(4, 12):
         node_right[node] = right_form(node_points[node])
 
@@ -311,15 +340,6 @@
     share = top_points.at[core, group]
     for step in range(1, TOPS):
         start(share, share, tpts_send.at[step], tpts_recv.at[step], peer(step))
-    for side, source, target, device in ((0, 8, 0, next_group), (1, 4, 12, previous_group)):
-        start(
-            node_points.at[pl.ds(source + 2 * core, 2)],
-            node_points.at[pl.ds(target + 2 * core, 2)],
-            edge_send.at[side],
-            edge_recv.at[side],
-            device,
-        )
-
     top_transfer = split(softmax3(exponents(upper_right[6], top_candidates)))
     for quad in range(2):
         half = slice(quad * RANK, (quad + 1) * RANK)
@@ -342,21 +362,30 @@
         ).wait_recv()
     start(node_values.at[pl.ds(8, 4)], node_values.at[pl.ds(0, 4)], edge_send.at[2], edge_recv.at[2], next_group)
     start(node_values.at[pl.ds(4, 4)], node_values.at[pl.ds(12, 4)], edge_send.at[3], edge_recv.at[3], previous_group)
+    pass_on(0)
+
     total = jnp.zeros((SHARE, RANK), F32)
     for node in range(GROUP):
         total = total + thin_product(nt, node_values[4 + node], (chain_high[node], chain_low[node]))
-    top_values[group] = total
+    top_share[...] = total.reshape(4, SHARE // 4, RANK)
     for step in range(1, TOPS):
-        start(top_values.at[group], top_values.at[group], tval_send.at[step], tval_recv.at[step], peer(step))
-
-    for here, paths in relays():
-
-        @pl.when(here)
-        def _():
-            for path in paths:
-                for arrived, copy in path:
-                    remote(*arrived).wait_recv()
-                    remote(*copy).start()
+        part = top_share.at[lax.rem(group + step, 4)]
+        start(part, top_values.at[group], tval_send.at[step], tval_recv.at[step], peer(step))
+    top_values[group] = top_share[quarter]
+
+    left_rows = jnp.concatenate([high, low, high, norms, ones, rest], axis=0)
+    for leaf in range(2):
+        rows = slice(leaf * LEAF, (leaf + 1) * LEAF)
+        leaf_left[rows, :] = jnp.transpose(left_rows[:, rows]).astype(BF16)
+        for half in range(2):
+            tile_rows, value = near_tile(leaf, half, 2 + leaf)
+            out[tile_rows, :] = value
+
+    for leaf in range(2):
+        rows = slice(leaf * LEAF, (leaf + 1) * LEAF)
+        basis_high[rows, :] = jnp.transpose(basis_t_high[:, rows].astype(F32)).astype(BF16)
+        basis_low[rows, :] = jnp.transpose(basis_t_low[:, rows].astype(F32)).astype(BF16)
+    pass_on(1)
 
     for side, target in ((0, 0), (1, 12)):
         landed = node_points.at[pl.ds(target + 2 * core, 2)]
@@ -400,19 +429,41 @@
 
     landed = top_points.at[1 - core]
     remote(landed, landed, tpts_send.at[0], tpts_recv.at[0], sibling).wait_recv()
-    tiles = []
-    for slot in range(FAR4):
-        source = top_far_list[slot, group]
-        tiles.append(split(jnp.exp2(exponents(right_form(top_points[:, source].reshape(FEAT, RANK)), upper_right[6]))))
+
+    def top_tiles(target, carry):
+        own = right_form(top_points[:, ring_first + target].reshape(FEAT, RANK))
+        for slot in range(FAR4):
+            source = top_far_list[slot, ring_first + target]
+            tile = jnp.exp2(exponents(right_form(top_points[:, source].reshape(FEAT, RANK)), own))
+            rows = slice(slot * RANK, (slot + 1) * RANK)
+            top_high[target, rows, :], top_low[target, rows, :] = split(tile)
+        return carry
+
+    lax.fori_loop(0, 4, top_tiles, 0, unroll=2)
     for step in range(1, TOPS):
-        source = lax.rem(group + TOPS - step, TOPS)
-        remote(
-            top_values.at[source], top_values.at[source], tval_send.at[step], tval_recv.at[step], peer(step)
-        ).wait_recv()
-    top_field = jnp.zeros((SHARE, RANK), F32)
-    for slot in range(FAR4):
-        source = top_far_list[slot, group]
-        top_field = top_field + thin_product(nn, top_values[source], tiles[slot])
+        landed = top_values.at[lax.rem(group + TOPS - step, TOPS)]
+        remote(landed, landed, tval_send.at[step], tval_recv.at[step], sibling).wait_recv()
+    for target in range(4):
+        values = jnp.concatenate(
+            [top_values[top_far_list[slot, ring_first + target]] for slot in range(FAR4)], axis=1
+        )
+        high = values.astype(BF16).astype(F32)
+        both = jnp.concatenate([high, values - high], axis=0).astype(BF16)
+        sums = nn(both, top_high[target]) + nn(both, top_low[target])
+        top_out[target] = sums[: SHARE // 4] + sums[SHARE // 4 :]
+    for step in range(1, 4):
+        start(
+            top_out.at[lax.rem(quarter + step, 4)],
+            top_in.at[quarter],
+            tout_send.at[step],
+            tout_recv.at[step],
+            ring(step),
+        )
+    top_in[quarter] = top_out[quarter]
+    for step in range(1, 4):
+        landed = top_in.at[lax.rem(quarter + 4 - step, 4)]
+        remote(landed, landed, tout_send.at[step], tout_recv.at[step], sibling).wait_recv()
+    top_field = top_in[...].reshape(SHARE, RANK)
     for node in range(GROUP):
         field_out[node] = field_out[node] + thin_product(nn, top_field, (chain_high[node], chain_low[node]))
     for step in range(1, GROUP):
@@ -459,11 +510,16 @@
         out[rows, :] = out[rows, :] + product3(nn, (basis_high[rows, :], basis_low[rows, :]), field)
     for copy in started:
         copy.wait_send()
-    for here, paths in relays():
-
-        @pl.when(here)
-        def _():
-            for path in paths:
+    for side in range(2):
+        for half in range(2):
+            for kind, landed in enumerate(near_refs(side, half)):
+                part = 2 * half + kind
+                remote(landed, landed, near_send.at[side, part], near_recv.at[side, part], sibling).wait_send()
+    for half in range(2):
+        for here, path in relays(half):
+
+            @pl.when(here)
+            def _():
                 for _, copy in path:
                     remote(*copy).wait_send()
 
@@ -496,7 +552,12 @@
             pltpu.VMEM((GROUP, 1, 128), jnp.int32),
             pltpu.SMEM((GROUP, 1, 128), jnp.int32),
             pltpu.VMEM((2, TOPS, FEAT // 2, RANK), F32),
-            pltpu.VMEM((TOPS, SHARE, RANK), F32),
+            pltpu.VMEM((TOPS, SHARE // 4, RANK), F32),
+            pltpu.VMEM((4, SHARE // 4, RANK), F32),
+            pltpu.VMEM((4, SHARE // 4, RANK), F32),
+            pltpu.VMEM((4, SHARE // 4, RANK), F32),
+            pltpu.VMEM((4, FAR4 * RANK, RANK), BF16),
+            pltpu.VMEM((4, FAR4 * RANK, RANK), BF16),
             pltpu.VMEM((GROUP, SHARE, RANK), F32),
             pltpu.VMEM((GROUP, SHARE, RANK), F32),
             pltpu.VMEM((GROUP, SHARE, RANK), F32),
@@ -527,6 +588,8 @@
             dma((TOPS,)),
             dma((TOPS,)),
             dma((TOPS,)),
+            dma((4,)),
+            dma((4,)),
             dma((GROUP,)),
             dma((GROUP,)),
             dma,

time: 55.2 us -> 51.7 us (0.937)
  the two profiles are of different devices: /device:TPU:2 before, /device:TPU:1 now
where the time goes in v3:
time: 51.7 us; the launch traced here: 51.5 us
  Pallas kernels  49.2 us (95%)
  local copies, waits for them, and re-layouts  2.26 us (4%)
    pallas_call x1, Pallas kernels, body(): pl.pallas_call(kernel, out_shape=jax.ShapeDtypeStruct((2 * LEAF, RHS), F3...  49.2 us
    unnamed x1, local copies, waits for them, and re-layouts  2.26 us

profile of v3, /device:TPU:1, one launch (start us, length us, event | category | flops | bytes accessed | tf_op | source)
XLA Modules:
  0.0 51.5 jit_solution(8823264777840227493)
XLA Ops:
  0.0 49.2 %shard_map.100 = f32[1024,256]{1,0:T(8,128)} custom-call(s32[2,3]{1,0:T(2,128)} %near_list.1, s32[1,3]{1,0:T(1,128)} %far_list.1, s32[3,16]{1,0:T(4,128)} %bitcast.3, f32[64,1024]{1,0:T(8,128)} %bitcast.2, f32[1024,256]{1,0:T(8,128)} %coefficients.1, s32[2,256]{1,0:T(2,128)} %leaf_skeleton.1, s32[1,256]{1,0:T(1,128)} %node_skeleton.1, ...), custom_call_target="tpu_custom_call" | custom-call | tf_op jit(solution)/shard_map/pallas_call | solution.py:542
  49.3 2.3 %copy.12 = f32[1024,256]{1,0:T(8,128)} copy(f32[1024,256]{1,0:T(8,128)} %shard_map.100) | data formatting | bytes 2097152

commit v4 on v3

--- a/solution.py
+++ b/solution.py
@@ -425,7 +425,6 @@
         landed = top_points.at[core, lax.rem(group + TOPS - step, TOPS)]
         remote(landed, landed, tpts_send.at[step], tpts_recv.at[step], sibling).wait_recv()
     start(top_points.at[core], top_points.at[core], tpts_send.at[0], tpts_recv.at[0], sibling)
-    lax.fori_loop(GROUP // 2, GROUP, far_node, 0, unroll=2)
 
     landed = top_points.at[1 - core]
     remote(landed, landed, tpts_send.at[0], tpts_recv.at[0], sibling).wait_recv()
@@ -460,6 +459,7 @@
             ring(step),
         )
     top_in[quarter] = top_out[quarter]
+    lax.fori_loop(GROUP // 2, GROUP, far_node, 0, unroll=2)
     for step in range(1, 4):
         landed = top_in.at[lax.rem(quarter + 4 - step, 4)]
         remote(landed, landed, tout_send.at[step], tout_recv.at[step], sibling).wait_recv()
@@ -476,12 +476,12 @@
         )
     field_in[place] = field_out[place]
 
-    for side in range(2):
-        for half in range(2):
-            for kind, landed in enumerate(near_refs(side, half)):
-                part = 2 * half + kind
+    for turn in range(2):
+        side = lax.rem(turn + first, 2)
+        for leaf in range(2):
+            for kind, landed in enumerate(near_refs(side, leaf)):
+                part = 2 * leaf + kind
                 remote(landed, landed, near_send.at[side, part], near_recv.at[side, part], sibling).wait_recv()
-        for leaf in range(2):
             slot = 4 * side + leaf
             rows = slice(leaf * LEAF, (leaf + 1) * LEAF)
             near_right[slot] = right_form(near_points[side, :, rows] * SCALE)

time: 51.7 us -> 51.7 us (level)
  no operation moved by 1% of the time
where the time goes in v4:
time: 51.7 us; the launch traced here: 51.5 us
  Pallas kernels  49.2 us (95%)
  local copies, waits for them, and re-layouts  2.26 us (4%)
    pallas_call x1, Pallas kernels, body(): pl.pallas_call(kernel, out_shape=jax.ShapeDtypeStruct((2 * LEAF, RHS), F3...  49.2 us
    unnamed x1, local copies, waits for them, and re-layouts  2.26 us

profile of v4, /device:TPU:1, one launch (start us, length us, event | category | flops | bytes accessed | tf_op | source)
XLA Modules:
  0.0 51.5 jit_solution(16781684597207084417)
XLA Ops:
  0.0 49.2 %shard_map.100 = f32[1024,256]{1,0:T(8,128)} custom-call(s32[2,3]{1,0:T(2,128)} %near_list.1, s32[1,3]{1,0:T(1,128)} %far_list.1, s32[3,16]{1,0:T(4,128)} %bitcast.3, f32[64,1024]{1,0:T(8,128)} %bitcast.2, f32[1024,256]{1,0:T(8,128)} %coefficients.1, s32[2,256]{1,0:T(2,128)} %leaf_skeleton.1, s32[1,256]{1,0:T(1,128)} %node_skeleton.1, ...), custom_call_target="tpu_custom_call" | custom-call | tf_op jit(solution)/shard_map/pallas_call | solution.py:542
  49.2 2.3 %copy.12 = f32[1024,256]{1,0:T(8,128)} copy(f32[1024,256]{1,0:T(8,128)} %shard_map.100) | data formatting | bytes 2097152
